TPU v7x, 32 devices: a whole 2x2x4 slice. The times are simulated.
32 devices in a mesh: ctx: 8 (over y, x, core), section: 4 (over z).
Axes of the slice: x: 2, y: 2, z: 4, core: 2. Of those that a mesh axis runs over, the one named last changes fastest.
Arguments:
- query_in: bfloat16 [4, 4, 8192], P('section', None, 'ctx'), may hold values from -100 to 100
- keys: bfloat16 [4, 4, 8192, 4, 128], P('section', None, 'ctx'), may hold values from -6 to 6
- values: bfloat16 [4, 4, 8192, 4, 128], P('section', None, 'ctx'), may hold values from -6 to 6
- lengths: int32 [4, 8], P(None, 'ctx'), may hold values from 256 to 1024, as said below
Outputs:
- attended: bfloat16 [4, 4, 8192], P('section', None, 'ctx')
Inputs may be any that keep to these rules, and one draw needn't show every extreme that they name: `lengths`: each request has one slab with all 1024 positions live.
All inputs are finite; a program needn't handle non-finite values.
Results may differ from a plain program's by a relative error of at most 0.028.
Values may be sent and summed in bfloat16 or wider, within the bound.
A program may use at most 64 MiB of HBM per device.

v0:
```python
import math

import jax
import jax.numpy as jnp
from jax import lax
from jax.sharding import PartitionSpec as P


def combined_all(value, axis, join):
    pieces = jax.tree.map(lambda part: lax.all_gather(part, axis), value)
    head = jax.tree.map(lambda part: part[0], pieces)
    tail = jax.tree.map(lambda part: part[1:], pieces)
    subtotal, _ = lax.scan(lambda subtotal, share: (join(subtotal, share), None), head, tail)
    return subtotal


def from_behind(value, axis, by):
    size = lax.axis_size(axis)
    pairs = [(i, i + by) for i in range(size) if 0 <= i + by < size]
    return lax.ppermute(value, axis, pairs)


def combine_states(earlier, later):
    joint_peak = jnp.maximum(earlier[0], later[0])
    left_scale = jnp.exp(earlier[0] - joint_peak)
    right_scale = jnp.exp(later[0] - joint_peak)
    return (
        joint_peak,
        earlier[1] * left_scale + later[1] * right_scale,
        earlier[2] * left_scale[..., None] + later[2] * right_scale[..., None],
    )


def body(query_in, keys, values, lengths):
    sections = lax.axis_size("section")
    slab_count = lax.axis_size("ctx")
    section_idx = lax.axis_index("section")
    slab_idx = lax.axis_index("ctx")
    requests = keys.shape[1]
    span = keys.shape[2]
    kv_heads = keys.shape[3]
    head_dim = keys.shape[4]
    row_width = query_in.shape[2]
    own_heads = row_width // head_dim
    group_size = own_heads * slab_count // kv_heads
    score_scale = 1.0 / math.sqrt(head_dim)
    positions = jnp.arange(span, dtype=jnp.int32)
    key_rows = keys[0]
    value_rows = values[0]
    prompts = query_in[0]

    def attend(query_rows, first_req, req_count):
        slab_keys = lax.dynamic_slice_in_dim(key_rows, first_req, req_count, 0)
        slab_values = lax.dynamic_slice_in_dim(value_rows, first_req, req_count, 0)
        live_mask = positions[None, :] < lax.dynamic_slice_in_dim(lengths, first_req, req_count, 0)
        all_queries = lax.all_gather(query_rows, "ctx", axis=1, tiled=True)
        grouped = all_queries.reshape(req_count, kv_heads, group_size, head_dim)
        scores = (
            jnp.einsum("rgqd,rtgd->rgqt", grouped, slab_keys, preferred_element_type=jnp.float32)
            * score_scale
        )
        scores = jnp.where(live_mask[:, None, None, :], scores, -jnp.inf)
        row_peak = jnp.max(scores, axis=-1)
        weights = jnp.exp(scores - row_peak[..., None])
        row_total = jnp.sum(weights, axis=-1)
        summed = jnp.einsum(
            "rgqt,rtgd->rgqd",
            weights.astype(jnp.bfloat16),
            slab_values,
            preferred_element_type=jnp.float32,
        )
        row_peak, row_total, summed = combined_all(
            (row_peak, row_total, summed), "ctx", combine_states
        )
        result = (summed / row_total[..., None]).reshape(
            req_count, own_heads * slab_count * head_dim
        )
        return lax.dynamic_slice_in_dim(result, slab_idx * row_width, row_width, 1)

    def step_one(turn_no, carried):
        incoming, results = carried
        request = turn_no - section_idx
        active_row = (request >= 0) & (request < requests)
        which_req = jnp.clip(request, 0, requests - 1)
        prompt = lax.dynamic_slice_in_dim(prompts, which_req, 1, 0)
        query_rows = (prompt.astype(jnp.float32) + incoming).astype(jnp.bfloat16)
        output = attend(query_rows, which_req, 1)
        updated = lax.dynamic_update_slice_in_dim(results, output, which_req, 0)
        results = jnp.where(active_row, updated, results)
        passed = from_behind(incoming + output, "section", 1)
        return (passed, results)

    initial = (
        jnp.zeros((1, row_width), jnp.float32),
        jnp.zeros((requests, row_width), jnp.float32),
    )
    unused, results = lax.fori_loop(0, requests + sections - 1, step_one, initial)
    return results.astype(jnp.bfloat16)[None]


def solution(mesh):
    return jax.shard_map(
        body,
        mesh=mesh,
        in_specs=(
            P("section", None, "ctx"),
            P("section", None, "ctx", None, None),
            P("section", None, "ctx", None, None),
            P(None, "ctx"),
        ),
        out_specs=P("section", None, "ctx"),
        check_vma=False,
    )
```

profile of v0, /device:TPU:25, one launch (start us, length us, event | category | flops | bytes accessed | tf_op | source)
XLA Modules:
  0.0 328.4 jit_solution(15266092772510539938)
XLA Ops:
  0.0 6.5 %copy_bitcast_fusion = (bf16[4,1024,4,128]{3,1,2,0:T(8,128)(2,1)}, bf16[4,1024,4,128]{3,1,2,0:T(8,128)(2,1)}) fusion(bf16[1,4,1024,4,128]{4,3,2,1,0:T(4,128)(2,1)} %param.10, bf16[1,4,1024,4,128]{4,3,2,1,0:T(4,128)(2,1)} %param.9), kind=kLoop, calls=%fused_computation.33 | loop fusion | bytes 16777216 | tf_op jit(solution)/shard_map/squeeze | solution.py:49
  6.6 321.2 %while.58 = (s32[]{:T(128)}, f32[1,1024]{1,0:T(1,128)S(1)}, bf16[4,1024]{1,0:T(4,128)(2,1)S(1)}, s32[]{:T(128)}, s32[4,1]{0,1:T(1,128)S(1)}, /*index=5*/bf16[4,1...) while((s32[]{:T(128)}, f32[1,1024]{1,0:T(1,128)S(1)}, ...), condition=%wide.region_5.6_spmd.clone, body=%wide.region_0.5_spmd.clone.sunk | while | flops 34052424 | bytes 4034510 | solution.py:97
  8.0 9.6 %all_gather.65 = bf16[1,8192]{1,0:T(2,128)(2,1)S(1)} all-gather(bf16[1,1024]{1,0:T(2,128)(2,1)S(1)} %add_convert_fusion.2), channel_id=1, replica_groups=mesh['ctx'=8,'section'=4] {'ctx'}, dimensions={1}, use_global_device_ids=true | all-gather | bytes 18432 | tf_op jit(solution)/shard_map/while/body/eval_jaxpr/all_gather | solution.py:56
  19.5 8.9 %all-gather.12 = f32[8,4,16]{2,1,0:T(4,128)S(1)} all-gather(f32[1,4,16]{2,1,0:T(4,128)S(1)} %bitcast.98), channel_id=3, replica_groups=mesh['ctx'=8,'section'=4] {'ctx'}, dimensions={0}, use_global_device_ids=true | all-gather | bytes 2304 | tf_op jit(solution)/shard_map/while/body/eval_jaxpr/all_gather | solution.py:10
  28.4 7.9 %all-gather.11 = f32[8,4,16]{2,1,0:T(4,128)S(1)} all-gather(f32[1,4,16]{2,1,0:T(4,128)S(1)} %bitcast.97), channel_id=2, replica_groups=mesh['ctx'=8,'section'=4] {'ctx'}, dimensions={0}, use_global_device_ids=true | all-gather | bytes 2304 | tf_op jit(solution)/shard_map/while/body/eval_jaxpr/all_gather | solution.py:10
  37.9 9.3 %all-gather.13 = f32[32,16,128]{2,1,0:T(8,128)S(1)} all-gather(f32[4,16,128]{2,1,0:T(8,128)S(1)} %fusion.35), channel_id=4, replica_groups=mesh['ctx'=8,'section'=4] {'ctx'}, dimensions={0}, use_global_device_ids=true | all-gather | bytes 294912 | tf_op jit(solution)/shard_map/while/body/eval_jaxpr/all_gather | solution.py:10
  49.8 3.0 collective-permute-done
  54.1 9.2 %all_gather.65 = bf16[1,8192]{1,0:T(2,128)(2,1)S(1)} all-gather(bf16[1,1024]{1,0:T(2,128)(2,1)S(1)} %add_convert_fusion.2), channel_id=1, replica_groups=mesh['ctx'=8,'section'=4] {'ctx'}, dimensions={1}, use_global_device_ids=true | all-gather | bytes 18432 | tf_op jit(solution)/shard_map/while/body/eval_jaxpr/all_gather | solution.py:56
  65.3 8.9 %all-gather.12 = f32[8,4,16]{2,1,0:T(4,128)S(1)} all-gather(f32[1,4,16]{2,1,0:T(4,128)S(1)} %bitcast.98), channel_id=3, replica_groups=mesh['ctx'=8,'section'=4] {'ctx'}, dimensions={0}, use_global_device_ids=true | all-gather | bytes 2304 | tf_op jit(solution)/shard_map/while/body/eval_jaxpr/all_gather | solution.py:10
  74.2 7.9 %all-gather.11 = f32[8,4,16]{2,1,0:T(4,128)S(1)} all-gather(f32[1,4,16]{2,1,0:T(4,128)S(1)} %bitcast.97), channel_id=2, replica_groups=mesh['ctx'=8,'section'=4] {'ctx'}, dimensions={0}, use_global_device_ids=true | all-gather | bytes 2304 | tf_op jit(solution)/shard_map/while/body/eval_jaxpr/all_gather | solution.py:10
  83.7 9.3 %all-gather.13 = f32[32,16,128]{2,1,0:T(8,128)S(1)} all-gather(f32[4,16,128]{2,1,0:T(8,128)S(1)} %fusion.35), channel_id=4, replica_groups=mesh['ctx'=8,'section'=4] {'ctx'}, dimensions={0}, use_global_device_ids=true | all-gather | bytes 294912 | tf_op jit(solution)/shard_map/while/body/eval_jaxpr/all_gather | solution.py:10
  95.7 3.0 collective-permute-done
  100.0 9.2 %all_gather.65 = bf16[1,8192]{1,0:T(2,128)(2,1)S(1)} all-gather(bf16[1,1024]{1,0:T(2,128)(2,1)S(1)} %add_convert_fusion.2), channel_id=1, replica_groups=mesh['ctx'=8,'section'=4] {'ctx'}, dimensions={1}, use_global_device_ids=true | all-gather | bytes 18432 | tf_op jit(solution)/shard_map/while/body/eval_jaxpr/all_gather | solution.py:56
  111.2 8.9 %all-gather.12 = f32[8,4,16]{2,1,0:T(4,128)S(1)} all-gather(f32[1,4,16]{2,1,0:T(4,128)S(1)} %bitcast.98), channel_id=3, replica_groups=mesh['ctx'=8,'section'=4] {'ctx'}, dimensions={0}, use_global_device_ids=true | all-gather | bytes 2304 | tf_op jit(solution)/shard_map/while/body/eval_jaxpr/all_gather | solution.py:10
  120.1 7.9 %all-gather.11 = f32[8,4,16]{2,1,0:T(4,128)S(1)} all-gather(f32[1,4,16]{2,1,0:T(4,128)S(1)} %bitcast.97), channel_id=2, replica_groups=mesh['ctx'=8,'section'=4] {'ctx'}, dimensions={0}, use_global_device_ids=true | all-gather | bytes 2304 | tf_op jit(solution)/shard_map/while/body/eval_jaxpr/all_gather | solution.py:10
  129.5 9.3 %all-gather.13 = f32[32,16,128]{2,1,0:T(8,128)S(1)} all-gather(f32[4,16,128]{2,1,0:T(8,128)S(1)} %fusion.35), channel_id=4, replica_groups=mesh['ctx'=8,'section'=4] {'ctx'}, dimensions={0}, use_global_device_ids=true | all-gather | bytes 294912 | tf_op jit(solution)/shard_map/while/body/eval_jaxpr/all_gather | solution.py:10
  145.8 9.2 %all_gather.65 = bf16[1,8192]{1,0:T(2,128)(2,1)S(1)} all-gather(bf16[1,1024]{1,0:T(2,128)(2,1)S(1)} %add_convert_fusion.2), channel_id=1, replica_groups=mesh['ctx'=8,'section'=4] {'ctx'}, dimensions={1}, use_global_device_ids=true | all-gather | bytes 18432 | tf_op jit(solution)/shard_map/while/body/eval_jaxpr/all_gather | solution.py:56
  157.0 8.9 %all-gather.12 = f32[8,4,16]{2,1,0:T(4,128)S(1)} all-gather(f32[1,4,16]{2,1,0:T(4,128)S(1)} %bitcast.98), channel_id=3, replica_groups=mesh['ctx'=8,'section'=4] {'ctx'}, dimensions={0}, use_global_device_ids=true | all-gather | bytes 2304 | tf_op jit(solution)/shard_map/while/body/eval_jaxpr/all_gather | solution.py:10
  165.9 7.9 %all-gather.11 = f32[8,4,16]{2,1,0:T(4,128)S(1)} all-gather(f32[1,4,16]{2,1,0:T(4,128)S(1)} %bitcast.97), channel_id=2, replica_groups=mesh['ctx'=8,'section'=4] {'ctx'}, dimensions={0}, use_global_device_ids=true | all-gather | bytes 2304 | tf_op jit(solution)/shard_map/while/body/eval_jaxpr/all_gather | solution.py:10
  175.4 9.3 %all-gather.13 = f32[32,16,128]{2,1,0:T(8,128)S(1)} all-gather(f32[4,16,128]{2,1,0:T(8,128)S(1)} %fusion.35), channel_id=4, replica_groups=mesh['ctx'=8,'section'=4] {'ctx'}, dimensions={0}, use_global_device_ids=true | all-gather | bytes 294912 | tf_op jit(solution)/shard_map/while/body/eval_jaxpr/all_gather | solution.py:10
  191.7 9.2 %all_gather.65 = bf16[1,8192]{1,0:T(2,128)(2,1)S(1)} all-gather(bf16[1,1024]{1,0:T(2,128)(2,1)S(1)} %add_convert_fusion.2), channel_id=1, replica_groups=mesh['ctx'=8,'section'=4] {'ctx'}, dimensions={1}, use_global_device_ids=true | all-gather | bytes 18432 | tf_op jit(solution)/shard_map/while/body/eval_jaxpr/all_gather | solution.py:56
  202.9 8.9 %all-gather.12 = f32[8,4,16]{2,1,0:T(4,128)S(1)} all-gather(f32[1,4,16]{2,1,0:T(4,128)S(1)} %bitcast.98), channel_id=3, replica_groups=mesh['ctx'=8,'section'=4] {'ctx'}, dimensions={0}, use_global_device_ids=true | all-gather | bytes 2304 | tf_op jit(solution)/shard_map/while/body/eval_jaxpr/all_gather | solution.py:10
  211.8 7.9 %all-gather.11 = f32[8,4,16]{2,1,0:T(4,128)S(1)} all-gather(f32[1,4,16]{2,1,0:T(4,128)S(1)} %bitcast.97), channel_id=2, replica_groups=mesh['ctx'=8,'section'=4] {'ctx'}, dimensions={0}, use_global_device_ids=true | all-gather | bytes 2304 | tf_op jit(solution)/shard_map/while/body/eval_jaxpr/all_gather | solution.py:10
  221.2 9.3 %all-gather.13 = f32[32,16,128]{2,1,0:T(8,128)S(1)} all-gather(f32[4,16,128]{2,1,0:T(8,128)S(1)} %fusion.35), channel_id=4, replica_groups=mesh['ctx'=8,'section'=4] {'ctx'}, dimensions={0}, use_global_device_ids=true | all-gather | bytes 294912 | tf_op jit(solution)/shard_map/while/body/eval_jaxpr/all_gather | solution.py:10
  237.5 9.2 %all_gather.65 = bf16[1,8192]{1,0:T(2,128)(2,1)S(1)} all-gather(bf16[1,1024]{1,0:T(2,128)(2,1)S(1)} %add_convert_fusion.2), channel_id=1, replica_groups=mesh['ctx'=8,'section'=4] {'ctx'}, dimensions={1}, use_global_device_ids=true | all-gather | bytes 18432 | tf_op jit(solution)/shard_map/while/body/eval_jaxpr/all_gather | solution.py:56
  248.7 8.9 %all-gather.12 = f32[8,4,16]{2,1,0:T(4,128)S(1)} all-gather(f32[1,4,16]{2,1,0:T(4,128)S(1)} %bitcast.98), channel_id=3, replica_groups=mesh['ctx'=8,'section'=4] {'ctx'}, dimensions={0}, use_global_device_ids=true | all-gather | bytes 2304 | tf_op jit(solution)/shard_map/while/body/eval_jaxpr/all_gather | solution.py:10
  257.6 7.9 %all-gather.11 = f32[8,4,16]{2,1,0:T(4,128)S(1)} all-gather(f32[1,4,16]{2,1,0:T(4,128)S(1)} %bitcast.97), channel_id=2, replica_groups=mesh['ctx'=8,'section'=4] {'ctx'}, dimensions={0}, use_global_device_ids=true | all-gather | bytes 2304 | tf_op jit(solution)/shard_map/while/body/eval_jaxpr/all_gather | solution.py:10
  267.0 9.3 %all-gather.13 = f32[32,16,128]{2,1,0:T(8,128)S(1)} all-gather(f32[4,16,128]{2,1,0:T(8,128)S(1)} %fusion.35), channel_id=4, replica_groups=mesh['ctx'=8,'section'=4] {'ctx'}, dimensions={0}, use_global_device_ids=true | all-gather | bytes 294912 | tf_op jit(solution)/shard_map/while/body/eval_jaxpr/all_gather | solution.py:10
  283.3 9.2 %all_gather.65 = bf16[1,8192]{1,0:T(2,128)(2,1)S(1)} all-gather(bf16[1,1024]{1,0:T(2,128)(2,1)S(1)} %add_convert_fusion.2), channel_id=1, replica_groups=mesh['ctx'=8,'section'=4] {'ctx'}, dimensions={1}, use_global_device_ids=true | all-gather | bytes 18432 | tf_op jit(solution)/shard_map/while/body/eval_jaxpr/all_gather | solution.py:56
  294.5 8.9 %all-gather.12 = f32[8,4,16]{2,1,0:T(4,128)S(1)} all-gather(f32[1,4,16]{2,1,0:T(4,128)S(1)} %bitcast.98), channel_id=3, replica_groups=mesh['ctx'=8,'section'=4] {'ctx'}, dimensions={0}, use_global_device_ids=true | all-gather | bytes 2304 | tf_op jit(solution)/shard_map/while/body/eval_jaxpr/all_gather | solution.py:10
  303.4 7.9 %all-gather.11 = f32[8,4,16]{2,1,0:T(4,128)S(1)} all-gather(f32[1,4,16]{2,1,0:T(4,128)S(1)} %bitcast.97), channel_id=2, replica_groups=mesh['ctx'=8,'section'=4] {'ctx'}, dimensions={0}, use_global_device_ids=true | all-gather | bytes 2304 | tf_op jit(solution)/shard_map/while/body/eval_jaxpr/all_gather | solution.py:10
  312.9 9.3 %all-gather.13 = f32[32,16,128]{2,1,0:T(8,128)S(1)} all-gather(f32[4,16,128]{2,1,0:T(8,128)S(1)} %fusion.35), channel_id=4, replica_groups=mesh['ctx'=8,'section'=4] {'ctx'}, dimensions={0}, use_global_device_ids=true | all-gather | bytes 294912 | tf_op jit(solution)/shard_map/while/body/eval_jaxpr/all_gather | solution.py:10
  (342 shorter events, 73.9 us)
Async XLA Ops:
  0.0 6.6 %copy-start.1 = (bf16[1,4,1024]{2,1,0:T(4,128)(2,1)S(1)}, bf16[1,4,1024]{2,1,0:T(4,128)(2,1)}, u32[]{:S(2)}) copy-start(bf16[1,4,1024]{2,1,0:T(4,128)(2,1)} %param.8) | copy-start | bytes 24580
  0.0 6.6 %copy-start.2 = (s32[4,1]{0,1:T(1,128)S(1)}, s32[4,1]{0,1:T(1,128)}, u32[]{:S(2)}) copy-start(s32[4,1]{0,1:T(1,128)} %param.11) | copy-start | bytes 52
  48.4 4.4 %collective-permute-start = (f32[1,1024]{1,0:T(1,128)S(1)}, f32[1,1024]{1,0:T(1,128)S(1)}, u32[]{:S(2)}, u32[]{:S(2)}) collective-permute-start(f32[1,1024]{1,0:T(1,128)S(1)} %dynamic-slice_add_fusion.2), channel_id=1, source_target_pairs={{0,1},{1,2},{2,3},{4,5},{5,6},{6,7},{8,9},{9,10},{10,11},{12,13},{... | collective-permute-start | bytes 12296 | tf_op jit(solution)/shard_map/while/body/eval_jaxpr/ppermute | solution.py:20
  94.3 4.4 %collective-permute-start = (f32[1,1024]{1,0:T(1,128)S(1)}, f32[1,1024]{1,0:T(1,128)S(1)}, u32[]{:S(2)}, u32[]{:S(2)}) collective-permute-start(f32[1,1024]{1,0:T(1,128)S(1)} %dynamic-slice_add_fusion.2), channel_id=1, source_target_pairs={{0,1},{1,2},{2,3},{4,5},{5,6},{6,7},{8,9},{9,10},{10,11},{12,13},{... | collective-permute-start | bytes 12296 | tf_op jit(solution)/shard_map/while/body/eval_jaxpr/ppermute | solution.py:20
  140.1 4.4 %collective-permute-start = (f32[1,1024]{1,0:T(1,128)S(1)}, f32[1,1024]{1,0:T(1,128)S(1)}, u32[]{:S(2)}, u32[]{:S(2)}) collective-permute-start(f32[1,1024]{1,0:T(1,128)S(1)} %dynamic-slice_add_fusion.2), channel_id=1, source_target_pairs={{0,1},{1,2},{2,3},{4,5},{5,6},{6,7},{8,9},{9,10},{10,11},{12,13},{... | collective-permute-start | bytes 12296 | tf_op jit(solution)/shard_map/while/body/eval_jaxpr/ppermute | solution.py:20
  186.0 4.4 %collective-permute-start = (f32[1,1024]{1,0:T(1,128)S(1)}, f32[1,1024]{1,0:T(1,128)S(1)}, u32[]{:S(2)}, u32[]{:S(2)}) collective-permute-start(f32[1,1024]{1,0:T(1,128)S(1)} %dynamic-slice_add_fusion.2), channel_id=1, source_target_pairs={{0,1},{1,2},{2,3},{4,5},{5,6},{6,7},{8,9},{9,10},{10,11},{12,13},{... | collective-permute-start | bytes 12296 | tf_op jit(solution)/shard_map/while/body/eval_jaxpr/ppermute | solution.py:20
  231.8 4.4 %collective-permute-start = (f32[1,1024]{1,0:T(1,128)S(1)}, f32[1,1024]{1,0:T(1,128)S(1)}, u32[]{:S(2)}, u32[]{:S(2)}) collective-permute-start(f32[1,1024]{1,0:T(1,128)S(1)} %dynamic-slice_add_fusion.2), channel_id=1, source_target_pairs={{0,1},{1,2},{2,3},{4,5},{5,6},{6,7},{8,9},{9,10},{10,11},{12,13},{... | collective-permute-start | bytes 12296 | tf_op jit(solution)/shard_map/while/body/eval_jaxpr/ppermute | solution.py:20
  277.6 4.4 %collective-permute-start = (f32[1,1024]{1,0:T(1,128)S(1)}, f32[1,1024]{1,0:T(1,128)S(1)}, u32[]{:S(2)}, u32[]{:S(2)}) collective-permute-start(f32[1,1024]{1,0:T(1,128)S(1)} %dynamic-slice_add_fusion.2), channel_id=1, source_target_pairs={{0,1},{1,2},{2,3},{4,5},{5,6},{6,7},{8,9},{9,10},{10,11},{12,13},{... | collective-permute-start | bytes 12296 | tf_op jit(solution)/shard_map/while/body/eval_jaxpr/ppermute | solution.py:20
  323.5 4.4 %collective-permute-start = (f32[1,1024]{1,0:T(1,128)S(1)}, f32[1,1024]{1,0:T(1,128)S(1)}, u32[]{:S(2)}, u32[]{:S(2)}) collective-permute-start(f32[1,1024]{1,0:T(1,128)S(1)} %dynamic-slice_add_fusion.2), channel_id=1, source_target_pairs={{0,1},{1,2},{2,3},{4,5},{5,6},{6,7},{8,9},{9,10},{10,11},{12,13},{... | collective-permute-start | bytes 12296 | tf_op jit(solution)/shard_map/while/body/eval_jaxpr/ppermute | solution.py:20
  327.8 0.6 copy-start
where the time goes:
time: 331 us; the launch traced here: 328 us
  blocking collectives  248 us (75%)
  matrix products  22.6 us (7%)
  waiting for transfers between devices  20.7 us (6%)
  other arithmetic  13.7 us (4%)
  local copies, waits for them, and re-layouts  12.4 us (4%)
  starting transfers between devices  9.04 us (3%)
    all_gather x21, blocking collectives, combined_all(): pieces = jax.tree.map(lambda part: lax.all_gather(part, axis), value)  183 us
    all_gather x7, blocking collectives, attend(): all_queries = lax.all_gather(query_rows, 'ctx', axis=1, tiled=True)  64.9 us
    ppermute x7, waiting for transfers between devices, from_behind(): return lax.ppermute(value, axis, pairs)  20.7 us
    dot_general x7, matrix products, attend(): jnp.einsum('rgqd,rtgd->rgqt', grouped, slab_keys, preferred_element_type=...  11.8 us
    dot_general x7, matrix products, attend(): jnp.einsum('rgqt,rtgd->rgqd', weights.astype(jnp.bfloat16), slab_values,...  10.8 us
    ppermute x7, starting transfers between devices, from_behind(): return lax.ppermute(value, axis, pairs)  9.04 us
  transfers between devices with their start and end apart: 7, of which 7 were waited for; matrix products, arithmetic and copies ran while one was open for 0% of the time, Pallas kernels for 0%

commit v1 on v0

v1 whole, which is shorter than its diff:
```python
import functools
import math

import jax
import jax.numpy as jnp
from jax import lax
from jax.experimental import pallas as pl
from jax.experimental.pallas import tpu as pltpu
from jax.sharding import PartitionSpec as P

MESH = pl.DeviceIdType.MESH
DEAD = -1e30
CHUNK = 512


def wait_bytes(ref, sem):
    pltpu.make_async_copy(ref, ref, sem).wait()


def kernel(
    dims, lengths, query, keys, values, out,
    key_buf, value_buf, bias, query_all, residual, state_out, state_in, hand_on, result,
    key_sem, value_sem, query_send, query_recv, state_send, state_recv, hand_send, hand_recv,
):
    slabs, sections, requests, own, kv_heads, span, head_dim, rows = dims
    ctx = lax.axis_index("ctx")
    section = lax.axis_index("section")
    heads = own * slabs
    group = heads // kv_heads
    width = span * kv_heads
    factor = math.log2(math.e) / math.sqrt(head_dim)
    has_next = section < sections - 1
    has_previous = section > 0
    before = jnp.maximum(section - 1, 0)
    after = jnp.minimum(section + 1, sections - 1)

    def load(r):
        return (
            pltpu.make_async_copy(keys.at[r], key_buf.at[r], key_sem.at[r]),
            pltpu.make_async_copy(values.at[r], value_buf.at[r], value_sem.at[r]),
        )

    barrier = pltpu.get_barrier_semaphore()
    for d in range(1, slabs):
        peer = lax.rem(ctx + d, slabs)
        pl.semaphore_signal(barrier, inc=1, device_id=(peer, section), device_id_type=MESH)

    @pl.when(has_previous)
    def _():
        for i in range(slabs):
            pl.semaphore_signal(barrier, inc=1, device_id=(i, before), device_id_type=MESH)

    for r in range(requests):
        for copy in load(r):
            copy.start()

    wide = query[...].astype(jnp.float32)
    for r in range(requests):
        for h in range(own):
            query_all[ctx, r, h : h + 1, :] = wide[r : r + 1, h * head_dim : (h + 1) * head_dim]

    pl.semaphore_wait(barrier, slabs - 1 + slabs * has_next.astype(jnp.int32))

    for d in range(1, slabs):
        peer = lax.rem(ctx + d, slabs)
        pltpu.make_async_remote_copy(
            src_ref=query_all.at[ctx], dst_ref=query_all.at[ctx],
            send_sem=query_send, recv_sem=query_recv,
            device_id=(peer, section), device_id_type=MESH,
        ).start()

    column = lax.broadcasted_iota(jnp.int32, (8, width), 1)
    for r in range(requests):
        alive = column < lengths[r] * kv_heads
        for g in range(kv_heads):
            bias[r, g] = jnp.where(alive & (lax.rem(column, kv_heads) == g), 0.0, DEAD)

    @pl.when(jnp.logical_not(has_previous))
    def _():
        residual[...] = jnp.zeros_like(residual)

    wait_bytes(query_all.at[pl.ds(0, slabs - 1)], query_recv)

    def attend(r):
        @pl.when(has_previous)
        def _():
            wait_bytes(residual.at[r], hand_recv.at[r])

        both = query_all[:, r] + residual[r]
        q = both[:, :own].reshape(heads, head_dim).astype(jnp.bfloat16)
        key_copy, value_copy = load(r)
        key_copy.wait()
        scores = []
        top = None
        for j in range(0, width, CHUNK):
            s = lax.dot_general(
                q, key_buf[r, j : j + CHUNK], (((1,), (1,)), ((), ())),
                preferred_element_type=jnp.float32,
            ) * factor
            s = s.reshape(kv_heads, group // 8, 8, CHUNK) + bias[r, :, :, j : j + CHUNK][:, None]
            s = s.reshape(heads, CHUNK)
            scores.append(s)
            top = s if top is None else jnp.maximum(top, s)
        peak = jnp.max(top, axis=-1, keepdims=True)
        value_copy.wait()
        mass = None
        mixed = None
        for n, j in enumerate(range(0, width, CHUNK)):
            w = jnp.exp2(scores[n] - peak)
            mass = w if mass is None else mass + w
            part = jnp.dot(
                w.astype(jnp.bfloat16), value_buf[r, j : j + CHUNK],
                preferred_element_type=jnp.float32,
            )
            mixed = part if mixed is None else mixed + part
        total = jnp.sum(mass, axis=-1, keepdims=True)
        mixed = mixed / total
        level = jnp.broadcast_to(peak + jnp.log2(total), (heads, head_dim))
        for i in range(slabs):
            state_out[r, i, 0, :own] = mixed[i * own : (i + 1) * own]
            state_out[r, i, 1, :own] = level[i * own : (i + 1) * own]
        for d in range(1, slabs):
            peer = lax.rem(ctx + d, slabs)
            pltpu.make_async_remote_copy(
                src_ref=state_out.at[r, peer], dst_ref=state_in.at[r, d - 1],
                send_sem=state_send.at[r], recv_sem=state_recv.at[r],
                device_id=(peer, section), device_id_type=MESH,
            ).start()

    def combine(r):
        wait_bytes(state_in.at[r], state_recv.at[r])
        parts = [state_out[r, ctx, 0, :own]] + [state_in[r, d, 0, :own] for d in range(slabs - 1)]
        levels = [state_out[r, ctx, 1, :own]] + [state_in[r, d, 1, :own] for d in range(slabs - 1)]
        top = functools.reduce(jnp.maximum, levels)
        shares = [jnp.exp2(level - top) for level in levels]
        mixed = sum(p * w for p, w in zip(parts, shares)) / sum(shares)

        @pl.when(has_next)
        def _():
            hand_on[r, :own] = residual[r, ctx, :own] + mixed
            for i in range(slabs):
                pltpu.make_async_remote_copy(
                    src_ref=hand_on.at[r], dst_ref=residual.at[r, ctx],
                    send_sem=hand_send.at[r], recv_sem=hand_recv.at[r],
                    device_id=(i, after), device_id_type=MESH,
                ).start()

        result[r, :own] = mixed

    def turn(r, _):
        @pl.when(r < requests)
        def _():
            attend(jnp.minimum(r, requests - 1))

        @pl.when(r > 0)
        def _():
            combine(jnp.maximum(r - 1, 0))

        return 0

    lax.fori_loop(0, requests + 1, turn, 0)

    for r in range(requests):
        for h in range(own):
            out[r : r + 1, h * head_dim : (h + 1) * head_dim] = result[r, h : h + 1, :]

    wait_bytes(query_all.at[pl.ds(0, slabs - 1)], query_send)
    for r in range(requests):
        wait_bytes(state_in.at[r], state_send.at[r])

    @pl.when(has_next)
    def _():
        for r in range(requests):
            wait_bytes(residual.at[r], hand_send.at[r])


def body(query_in, keys, values, lengths):
    sections = lax.axis_size("section")
    slabs = lax.axis_size("ctx")
    _, requests, span, kv_heads, head_dim = keys.shape
    own = query_in.shape[2] // head_dim
    rows = -(-own // 8) * 8
    width = span * kv_heads
    dims = (slabs, sections, requests, own, kv_heads, span, head_dim, rows)
    flat_keys = keys.reshape(requests, width, head_dim)
    flat_values = values.reshape(requests, width, head_dim)
    dma = pltpu.SemaphoreType.DMA
    f32 = jnp.float32
    result = pl.pallas_call(
        functools.partial(kernel, dims),
        out_shape=jax.ShapeDtypeStruct((requests, own * head_dim), f32),
        in_specs=[
            pl.BlockSpec(memory_space=pltpu.SMEM),
            pl.BlockSpec(memory_space=pltpu.VMEM),
            pl.BlockSpec(memory_space=pltpu.HBM),
            pl.BlockSpec(memory_space=pltpu.HBM),
        ],
        out_specs=pl.BlockSpec(memory_space=pltpu.VMEM),
        scratch_shapes=[
            pltpu.VMEM((requests, width, head_dim), jnp.bfloat16),
            pltpu.VMEM((requests, width, head_dim), jnp.bfloat16),
            pltpu.VMEM((requests, kv_heads, 8, width), f32),
            pltpu.VMEM((slabs, requests, rows, head_dim), f32),
            pltpu.VMEM((requests, slabs, rows, head_dim), f32),
            pltpu.VMEM((requests, slabs, 2, rows, head_dim), f32),
            pltpu.VMEM((requests, slabs - 1, 2, rows, head_dim), f32),
            pltpu.VMEM((requests, rows, head_dim), f32),
            pltpu.VMEM((requests, rows, head_dim), f32),
            dma((requests,)),
            dma((requests,)),
            dma,
            dma,
            dma((requests,)),
            dma((requests,)),
            dma((requests,)),
            dma((requests,)),
        ],
        compiler_params=pltpu.CompilerParams(
            collective_id=0, has_side_effects=True, vmem_limit_bytes=60 * 1024 * 1024
        ),
        name="layered_decode",
    )(lengths[:, 0], query_in[0], flat_keys, flat_values)
    return result.astype(jnp.bfloat16)[None]


def solution(mesh):
    return jax.shard_map(
        body,
        mesh=mesh,
        in_specs=(
            P("section", None, "ctx"),
            P("section", None, "ctx", None, None),
            P("section", None, "ctx", None, None),
            P(None, "ctx"),
        ),
        out_specs=P("section", None, "ctx"),
        check_vma=False,
    )
```

time: 331 us -> 41.9 us (0.13)
  blocking collectives: 248 us -> 0 us
  Pallas kernels: 0 us -> 40.3 us
  matrix products: 22.6 us -> 0 us
  waiting for transfers between devices: 20.7 us -> 0 us
  local copies, waits for them, and re-layouts: 12.4 us -> 0 us
  other arithmetic: 13.7 us -> 1.32 us
  starting transfers between devices: 9.04 us -> 0 us
    all_gather x28 -> x0, blocking collectives: 248 us -> none  [the longest x21 183 us: combined_all(): pieces = jax.tree.map(lambda part: lax.all_gather(part, axis), value)]
    pallas_call x0 -> x1, Pallas kernels: none -> 40.3 us  [body(): pl.pallas_call(functools.partial(kernel, dims), out_shape=jax.ShapeDtypeS...]
    dot_general x14 -> x0, matrix products: 22.6 us -> none  [the longest x7 11.8 us: attend(): jnp.einsum('rgqd,rtgd->rgqt', grouped, slab_keys, preferred_element_type=...]
    ppermute x7 -> x0, waiting for transfers between devices: 20.7 us -> none  [from_behind(): return lax.ppermute(value, axis, pairs)]
    ppermute x7 -> x0, starting transfers between devices: 9.04 us -> none  [from_behind(): return lax.ppermute(value, axis, pairs)]
    squeeze x8 -> x0, local copies, waits for them, and re-layouts: 6.56 us -> none  [the longest x1 6.54 us: body(): value_rows = values[0]]
    lt x7 -> x0, other arithmetic: 4.75 us -> none  [attend(): positions[None, :]]
    dynamic_slice x7 -> x0, local copies, waits for them, and re-layouts: 4.53 us -> none  [attend(): lax.dynamic_slice_in_dim(lengths, first_req, req_count, 0)]
  transfers between devices with their start and end apart: 7 -> 0, of which waited for: 7 -> 0; matrix products, arithmetic and copies ran while one was open for 0% -> 0% of each run, Pallas kernels for 0% -> 0%
where the time goes in v1:
time: 41.9 us; the launch traced here: 41.6 us
  Pallas kernels  40.3 us (96%)
  other arithmetic  1.32 us (3%)
    pallas_call x1, Pallas kernels, body(): pl.pallas_call(functools.partial(kernel, dims), out_shape=jax.ShapeDtypeS...  40.3 us
    broadcast_in_dim x1, other arithmetic, body(): return result.astype(jnp.bfloat16)[None]  1.32 us

profile of v1, /device:TPU:25, one launch (start us, length us, event | category | flops | bytes accessed | tf_op | source)
XLA Modules:
  0.0 41.6 jit_solution(3013667861574592439)
XLA Ops:
  0.0 40.3 %layered_decode.1 = f32[4,1024]{1,0:T(4,128)} custom-call(s32[4]{0:T(128)} %bitcast.9, bf16[4,1024]{1,0:T(4,128)(2,1)} %bitcast.8, bf16[4,4096,128]{2,1,0:T(8,128)(2,1)} %bitcast.6, bf16[4,4096,128]{2,1,0:T(8,128)(2,1)} %bitcast.7), custom_call_target="tpu_custom_call" | custom-call | tf_op jit(solution)/shard_map/layered_decode/pallas_call | solution.py:189
  40.3 1.3 %convert_bitcast_fusion = bf16[1,4,1024]{2,1,0:T(4,128)(2,1)} fusion(f32[4,1024]{1,0:T(4,128)} %layered_decode.1), kind=kLoop, calls=%fused_computation | loop fusion | flops 4096 | bytes 24576 | tf_op jit(solution)/shard_map/broadcast_in_dim | solution.py:223

commit v2 on v1

--- a/solution.py
+++ b/solution.py
@@ -18,9 +18,9 @@
 
 
 def kernel(
-    dims, lengths, query, keys, values, out,
+    dims, lengths_in, query_in, keys, values, out, lengths, query,
     key_buf, value_buf, bias, query_all, residual, state_out, state_in, hand_on, result,
-    key_sem, value_sem, query_send, query_recv, state_send, state_recv, hand_send, hand_recv,
+    key_sem, value_sem, query_send, query_recv, state_send, state_recv, hand_send, hand_recv, small_sem,
 ):
     slabs, sections, requests, own, kv_heads, span, head_dim, rows = dims
     ctx = lax.axis_index("ctx")
@@ -50,9 +50,14 @@
         for i in range(slabs):
             pl.semaphore_signal(barrier, inc=1, device_id=(i, before), device_id_type=MESH)
 
+    query_copy = pltpu.make_async_copy(query_in, query, small_sem.at[0])
+    lengths_copy = pltpu.make_async_copy(lengths_in, lengths, small_sem.at[1])
+    query_copy.start()
+    lengths_copy.start()
     for r in range(requests):
         for copy in load(r):
             copy.start()
+    query_copy.wait()
 
     wide = query[...].astype(jnp.float32)
     for r in range(requests):
@@ -69,6 +74,7 @@
             device_id=(peer, section), device_id_type=MESH,
         ).start()
 
+    lengths_copy.wait()
     column = lax.broadcasted_iota(jnp.int32, (8, width), 1)
     for r in range(requests):
         alive = column < lengths[r] * kv_heads
@@ -147,18 +153,16 @@
 
         result[r, :own] = mixed
 
-    def turn(r, _):
-        @pl.when(r < requests)
-        def _():
-            attend(jnp.minimum(r, requests - 1))
-
-        @pl.when(r > 0)
-        def _():
-            combine(jnp.maximum(r - 1, 0))
-
+    def attend_turn(r, _):
+        attend(r)
         return 0
 
-    lax.fori_loop(0, requests + 1, turn, 0)
+    def combine_turn(r, _):
+        combine(r)
+        return 0
+
+    lax.fori_loop(0, requests, attend_turn, 0)
+    lax.fori_loop(0, requests, combine_turn, 0)
 
     for r in range(requests):
         for h in range(own):
@@ -190,13 +194,15 @@
         functools.partial(kernel, dims),
         out_shape=jax.ShapeDtypeStruct((requests, own * head_dim), f32),
         in_specs=[
-            pl.BlockSpec(memory_space=pltpu.SMEM),
-            pl.BlockSpec(memory_space=pltpu.VMEM),
+            pl.BlockSpec(memory_space=pltpu.HBM),
+            pl.BlockSpec(memory_space=pltpu.HBM),
             pl.BlockSpec(memory_space=pltpu.HBM),
             pl.BlockSpec(memory_space=pltpu.HBM),
         ],
         out_specs=pl.BlockSpec(memory_space=pltpu.VMEM),
         scratch_shapes=[
+            pltpu.SMEM((requests,), jnp.int32),
+            pltpu.VMEM((requests, own * head_dim), jnp.bfloat16),
             pltpu.VMEM((requests, width, head_dim), jnp.bfloat16),
             pltpu.VMEM((requests, width, head_dim), jnp.bfloat16),
             pltpu.VMEM((requests, kv_heads, 8, width), f32),
@@ -214,6 +220,7 @@
             dma((requests,)),
             dma((requests,)),
             dma((requests,)),
+            dma((2,)),
         ],
         compiler_params=pltpu.CompilerParams(
             collective_id=0, has_side_effects=True, vmem_limit_bytes=60 * 1024 * 1024

time: 41.9 us -> 38.5 us (0.919)
  Pallas kernels: 40.3 us -> 36.9 us
    pallas_call x1, Pallas kernels: 40.3 us -> 36.9 us  [body(): pl.pallas_call(functools.partial(kernel, dims), out_shape=jax.ShapeDtypeS...]
where the time goes in v2:
time: 38.5 us; the launch traced here: 38.3 us
  Pallas kernels  36.9 us (96%)
  other arithmetic  1.32 us (3%)
    pallas_call x1, Pallas kernels, body(): pl.pallas_call(functools.partial(kernel, dims), out_shape=jax.ShapeDtypeS...  36.9 us
    broadcast_in_dim x1, other arithmetic, body(): return result.astype(jnp.bfloat16)[None]  1.32 us

profile of v2, /device:TPU:25, one launch (start us, length us, event | category | flops | bytes accessed | tf_op | source)
XLA Modules:
  0.0 38.3 jit_solution(10635881752113859275)
XLA Ops:
  0.0 36.9 %layered_decode.1 = f32[4,1024]{1,0:T(4,128)} custom-call(s32[4]{0:T(128)} %bitcast.9, bf16[4,1024]{1,0:T(4,128)(2,1)} %bitcast.8, bf16[4,4096,128]{2,1,0:T(8,128)(2,1)} %bitcast.6, bf16[4,4096,128]{2,1,0:T(8,128)(2,1)} %bitcast.7), custom_call_target="tpu_custom_call" | custom-call | tf_op jit(solution)/shard_map/layered_decode/pallas_call | solution.py:193
  37.0 1.3 %convert_bitcast_fusion = bf16[1,4,1024]{2,1,0:T(4,128)(2,1)} fusion(f32[4,1024]{1,0:T(4,128)} %layered_decode.1), kind=kLoop, calls=%fused_computation | loop fusion | flops 4096 | bytes 24576 | tf_op jit(solution)/shard_map/broadcast_in_dim | solution.py:230

commit v3 on v2

--- a/solution.py
+++ b/solution.py
@@ -66,13 +66,17 @@
 
     pl.semaphore_wait(barrier, slabs - 1 + slabs * has_next.astype(jnp.int32))
 
-    for d in range(1, slabs):
-        peer = lax.rem(ctx + d, slabs)
-        pltpu.make_async_remote_copy(
-            src_ref=query_all.at[ctx], dst_ref=query_all.at[ctx],
-            send_sem=query_send, recv_sem=query_recv,
-            device_id=(peer, section), device_id_type=MESH,
-        ).start()
+    firsts = pl.ds(0, 1)
+    others = pl.ds(1, requests - 1)
+    arrivals = pl.ds(0, slabs - 1)
+    for part, span_of in enumerate((firsts, others)):
+        for d in range(1, slabs):
+            peer = lax.rem(ctx + d, slabs)
+            pltpu.make_async_remote_copy(
+                src_ref=query_all.at[ctx, span_of], dst_ref=query_all.at[ctx, span_of],
+                send_sem=query_send.at[part], recv_sem=query_recv.at[part],
+                device_id=(peer, section), device_id_type=MESH,
+            ).start()
 
     lengths_copy.wait()
     column = lax.broadcasted_iota(jnp.int32, (8, width), 1)
@@ -85,9 +89,13 @@
     def _():
         residual[...] = jnp.zeros_like(residual)
 
-    wait_bytes(query_all.at[pl.ds(0, slabs - 1)], query_recv)
+    wait_bytes(query_all.at[arrivals, firsts], query_recv.at[0])
 
     def attend(r):
+        @pl.when(r == 1)
+        def _():
+            wait_bytes(query_all.at[arrivals, others], query_recv.at[1])
+
         @pl.when(has_previous)
         def _():
             wait_bytes(residual.at[r], hand_recv.at[r])
@@ -168,7 +176,8 @@
         for h in range(own):
             out[r : r + 1, h * head_dim : (h + 1) * head_dim] = result[r, h : h + 1, :]
 
-    wait_bytes(query_all.at[pl.ds(0, slabs - 1)], query_send)
+    wait_bytes(query_all.at[arrivals, firsts], query_send.at[0])
+    wait_bytes(query_all.at[arrivals, others], query_send.at[1])
     for r in range(requests):
         wait_bytes(state_in.at[r], state_send.at[r])
 
@@ -214,8 +223,8 @@
             pltpu.VMEM((requests, rows, head_dim), f32),
             dma((requests,)),
             dma((requests,)),
-            dma,
-            dma,
+            dma((2,)),
+            dma((2,)),
             dma((requests,)),
             dma((requests,)),
             dma((requests,)),

time: 38.5 us -> 38 us (0.987)
  Pallas kernels: 36.9 us -> 36.5 us
    pallas_call x1, Pallas kernels: 36.9 us -> 36.5 us  [body(): pl.pallas_call(functools.partial(kernel, dims), out_shape=jax.ShapeDtypeS...]
where the time goes in v3:
time: 38 us; the launch traced here: 37.8 us
  Pallas kernels  36.5 us (96%)
  other arithmetic  1.32 us (3%)
    pallas_call x1, Pallas kernels, body(): pl.pallas_call(functools.partial(kernel, dims), out_shape=jax.ShapeDtypeS...  36.5 us
    broadcast_in_dim x1, other arithmetic, body(): return result.astype(jnp.bfloat16)[None]  1.32 us

profile of v3, /device:TPU:25, one launch (start us, length us, event | category | flops | bytes accessed | tf_op | source)
XLA Modules:
  0.0 37.8 jit_solution(15626829913515390659)
XLA Ops:
  0.0 36.5 %layered_decode.1 = f32[4,1024]{1,0:T(4,128)} custom-call(s32[4]{0:T(128)} %bitcast.9, bf16[4,1024]{1,0:T(4,128)(2,1)} %bitcast.8, bf16[4,4096,128]{2,1,0:T(8,128)(2,1)} %bitcast.6, bf16[4,4096,128]{2,1,0:T(8,128)(2,1)} %bitcast.7), custom_call_target="tpu_custom_call" | custom-call | tf_op jit(solution)/shard_map/layered_decode/pallas_call | solution.py:202
  36.5 1.3 %convert_bitcast_fusion = bf16[1,4,1024]{2,1,0:T(4,128)(2,1)} fusion(f32[4,1024]{1,0:T(4,128)} %layered_decode.1), kind=kLoop, calls=%fused_computation | loop fusion | flops 4096 | bytes 24576 | tf_op jit(solution)/shard_map/broadcast_in_dim | solution.py:239
